TPU v7x, 768 devices: a whole 4x8x12 slice. The times are simulated.
768 devices in a mesh: dp: 96 (over x, y_lo, z), group: 8 (over y_hi, core).
Axes of the slice: x: 4, y: 8 (y_hi: 4, y_lo: 2; y = y_hi * 2 + y_lo), z: 12, core: 2. Of those that a mesh axis runs over, the one named last changes fastest.
Arguments:
- image_emb: bfloat16 [196608, 1152], P(('dp', 'group')), may hold values from -0.17675781 to 0.17675781
- text_emb: float32 [196608, 1152], P(('dp', 'group')), may hold values from -0.17677669 to 0.17677669
- text_accum: float32 [196608, 1152], P(('dp', 'group')), may hold values from -6 to 6
- pair_ids: int32 [196608], P(('dp', 'group')), may hold values from 0 to 127
- log_scale: float32 [1], replicated, may hold values from 1 to 2
- bias: float32 [1], replicated, may hold values from -3 to 0
Outputs:
- row_loss: float32 [196608], P(('dp', 'group'))
- image_grad: bfloat16 [196608, 1152], P(('dp', 'group'))
- text_grad: float32 [196608, 1152], P(('dp', 'group'))
Inputs may be any that keep to these rules, and one draw needn't show every extreme that they name: `pair_ids`: two examples form a positive pair exactly where their ids are equal.
All inputs are finite; a program needn't handle non-finite values.
Results may differ from a plain program's by a relative error of at most 0.0059.
Values may be sent and summed in bfloat16 or wider, within the bound.
A program may use at most 32 MiB of HBM per device.

v0:
```python
import jax
import jax.numpy as jnp
from jax import lax
from jax.sharding import PartitionSpec as P

SHIFTS = 2


def from_behind(block, axis, distance):
    devices = range(lax.axis_size(axis))
    route = [((i - distance) % len(devices), i) for i in devices]
    return lax.ppermute(block, axis, route)


def block_terms(image_block, text_block, image_ids, text_ids, scale, shift):
    logits = (
        scale
        * lax.dot_general(
            image_block, text_block, (((1,), (1,)), ((), ())), preferred_element_type=jnp.float32
        )
        + shift
    )
    signs = jnp.where(image_ids[:, None] == text_ids[None, :], 1.0, -1.0).astype(jnp.float32)
    loss = jnp.sum(jax.nn.softplus(-signs * logits), axis=1)
    coef = (-signs * jax.nn.sigmoid(-signs * logits) * scale).astype(jnp.bfloat16)
    image_part = jnp.dot(coef, text_block, preferred_element_type=jnp.float32)
    text_part = lax.dot_general(
        coef, image_block, (((0,), (0,)), ((), ())), preferred_element_type=jnp.float32
    )
    return (loss, image_part, text_part)


def body(image_emb, text_emb, text_accum, pair_ids, log_scale, bias):
    scale = jnp.exp(log_scale[0])
    shift = bias[0]
    texts = text_emb.astype(jnp.bfloat16)
    loss, image_sum, text_part = block_terms(image_emb, texts, pair_ids, pair_ids, scale, shift)
    text_ids = pair_ids
    carried = text_accum + text_part
    for step in range(SHIFTS):
        texts = from_behind(texts, ("dp", "group"), 1)
        text_ids, carried = from_behind((text_ids, carried), ("dp", "group"), 1)
        part_loss, image_part, text_part = block_terms(
            image_emb, texts, pair_ids, text_ids, scale, shift
        )
        loss = loss + part_loss
        image_sum = image_sum + image_part
        carried = carried + text_part
    row_loss = loss / ((SHIFTS + 1) * image_emb.shape[0])
    return (row_loss, image_sum.astype(jnp.bfloat16), carried)


def solution(mesh):
    in_specs = (
        P(("dp", "group"), None),
        P(("dp", "group"), None),
        P(("dp", "group"), None),
        P(("dp", "group")),
        P(),
        P(),
    )
    out_specs = (P(("dp", "group")), P(("dp", "group"), None), P(("dp", "group"), None))
    return jax.shard_map(body, mesh=mesh, in_specs=in_specs, out_specs=out_specs, check_vma=False)
```

profile of v0, /device:TPU:62, one launch (start us, length us, event | category | flops | bytes accessed | tf_op | source)
XLA Modules:
  0.0 116.9 jit_solution(11800450731169113375)
XLA Ops:
  0.6 0.0 copy-start
  0.6 0.0 copy-start.2
  2.0 1.3 %convert_element_type.15 = bf16[256,1152]{1,0:T(8,128)(2,1)S(1)} convert(f32[256,1152]{1,0:T(8,128)} %param.7) | non-fusion elementwise | flops 294912 | bytes 1769472 | tf_op jit(solution)/shard_map/convert_element_type | solution.py:36
  3.4 0.0 copy-start.1
  3.4 0.0 copy-done
  3.4 0.0 copy-done.2
  3.4 0.5 fusion.7
  4.0 0.7 copy-done.1
  4.7 0.4 convolution_add_fusion.1
  5.1 1.9 %collective-permute-start.4 = (f32[256,1152]{1,0:T(8,128)S(1)}, f32[256,1152]{1,0:T(8,128)S(1)}, u32[]{:S(2)}, u32[]{:S(2)}) collective-permute-start(f32[256,1152]{1,0:T(8,128)S(1)} %convolution_add_fusion.1), channel_id=1, source_target_pairs={{767,0},{0,1},{1,2},{2,3},{3,4},{4,5},{5,6},{6,7},{7,8},{8,9},{9,1... | collective-permute-start | bytes 3538952 | tf_op jit(solution)/shard_map/ppermute | solution.py:12
  7.0 4.6 %collective-permute-start.1 = (bf16[256,1152]{1,0:T(8,128)(2,1)S(1)}, bf16[256,1152]{1,0:T(8,128)(2,1)S(1)}, u32[]{:S(2)}, u32[]{:S(2)}) collective-permute-start(bf16[256,1152]{1,0:T(8,128)(2,1)S(1)} %convert_element_type.15), channel_id=1, source_target_pairs={{767,0},{0,1},{1,2},{2,3},{3,4},{4,5},{5,6},{6,7},{7,8},{8,9},{9,1... | collective-permute-start | bytes 1769480 | tf_op jit(solution)/shard_map/ppermute | solution.py:12
  11.6 1.9 %collective-permute-start = (s32[256]{0:T(256)S(1)}, s32[256]{0:T(256)S(1)}, u32[]{:S(2)}, u32[]{:S(2)}) collective-permute-start(s32[256]{0:T(256)S(1)} %copy-done.2), channel_id=1, source_target_pairs={{767,0},{0,1},{1,2},{2,3},{3,4},{4,5},{5,6},{6,7},{7,8},{8,9},{9,1... | collective-permute-start | bytes 3080 | tf_op jit(solution)/shard_map/ppermute | solution.py:12
  13.5 63.4 %collective-permute-done.1 = bf16[256,1152]{1,0:T(8,128)(2,1)S(1)} collective-permute-done((bf16[256,1152]{1,0:T(8,128)(2,1)S(1)}, bf16[256,1152]{1,0:T(8,128)(2,1)S(1)}, u32[]{:S(2)}, u32[]{:S(2)}) %collective-permute-start.1) | collective-permute-done | bytes 589856 | tf_op jit(solution)/shard_map/ppermute | solution.py:12
  76.9 1.9 %collective-permute-start.3 = (bf16[256,1152]{1,0:T(8,128)(2,1)S(1)}, bf16[256,1152]{1,0:T(8,128)(2,1)S(1)}, u32[]{:S(2)}, u32[]{:S(2)}) collective-permute-start(bf16[256,1152]{1,0:T(8,128)(2,1)S(1)} %collective-permute-done.1), channel_id=1, source_target_pairs={{767,0},{0,1},{1,2},{2,3},{3,4},{4,5},{5,6},{6,7},{7,8},{8,9},{9,1... | collective-permute-start | bytes 1769480 | tf_op jit(solution)/shard_map/ppermute | solution.py:12
  78.8 0.0 collective-permute-done
  78.8 0.5 fusion.8
  79.3 0.0 collective-permute-done.4
  79.4 0.4 convolution_add_fusion
  79.8 1.9 %collective-permute-start.5 = (f32[256,1152]{1,0:T(8,128)S(1)}, f32[256,1152]{1,0:T(8,128)S(1)}, u32[]{:S(2)}, u32[]{:S(2)}) collective-permute-start(f32[256,1152]{1,0:T(8,128)S(1)} %convolution_add_fusion), channel_id=1, source_target_pairs={{767,0},{0,1},{1,2},{2,3},{3,4},{4,5},{5,6},{6,7},{7,8},{8,9},{9,1... | collective-permute-start | bytes 3538952 | tf_op jit(solution)/shard_map/ppermute | solution.py:12
  81.7 0.5 fusion.10
  82.2 1.9 %collective-permute-start.2 = (s32[256]{0:T(256)S(1)}, s32[256]{0:T(256)S(1)}, u32[]{:S(2)}, u32[]{:S(2)}) collective-permute-start(s32[256]{0:T(256)S(1)} %collective-permute-done), channel_id=1, source_target_pairs={{767,0},{0,1},{1,2},{2,3},{3,4},{4,5},{5,6},{6,7},{7,8},{8,9},{9,1... | collective-permute-start | bytes 3080 | tf_op jit(solution)/shard_map/ppermute | solution.py:12
  84.1 0.5 convolution_add_fusion.3
  84.6 28.5 %collective-permute-done.2 = s32[256]{0:T(256)S(1)} collective-permute-done((s32[256]{0:T(256)S(1)}, s32[256]{0:T(256)S(1)}, u32[]{:S(2)}, u32[]{:S(2)}) %collective-permute-start.2) | collective-permute-done | bytes 1056 | tf_op jit(solution)/shard_map/ppermute | solution.py:12
  113.1 0.0 collective-permute-done.3
  113.1 0.5 fusion.9
  113.6 0.6 add_multiply_fusion
  114.2 1.3 %fusion = bf16[256,1152]{1,0:T(8,128)(2,1)} fusion(f32[256,1152]{1,0:T(8,128)S(1)} %convolution_add_fusion.3, bf16[256,1152]{1,0:T(8,128)(2,1)S(1)} %collective-permute-done.3, f32[256,256]{0,1:T(8,128)S(1)} %get-tuple-element.4, f32[]{:T(128)} %bitcast, s32[256]{0:T(256)S(1)} %copy-done.2, s32[256]{0:T(256)S(1)} %collective-permute-done.2), kind=kOutput, calls=%fused_computation.4 | convolution fusion | flops 152174592 | bytes 2623492 | tf_op jit(solution)/shard_map/dot_general | solution.py:26
  115.5 0.0 collective-permute-done.5
  115.5 1.4 %fusion.12 = f32[256,1152]{1,0:T(8,128)} fusion(f32[256,1152]{1,0:T(8,128)S(1)} %collective-permute-done.5, bf16[256,1152]{1,0:T(8,128)(2,1)S(1)} %copy-done, f32[256,256]{0,1:T(8,128)S(1)} %get-tuple-element.4, f32[]{:T(128)} %bitcast, s32[256]{0:T(256)S(1)} %copy-done.2, s32[256]{0:T(256)S(1)} %collective-permute-done.2), kind=kOutput, calls=%fused_computation.29 | convolution fusion | flops 151879680 | bytes 3213316 | tf_op jit(solution)/shard_map/dot_general | solution.py:27
Async XLA Ops:
  0.6 2.8 %copy-start = (bf16[256,1152]{1,0:T(8,128)(2,1)S(1)}, bf16[256,1152]{1,0:T(8,128)(2,1)}, u32[]{:S(2)}) copy-start(bf16[256,1152]{1,0:T(8,128)(2,1)} %param.6) | copy-start | bytes 1769476
  0.6 2.8 %copy-start.2 = (s32[256]{0:T(256)S(1)}, s32[256]{0:T(256)}, u32[]{:S(2)}) copy-start(s32[256]{0:T(256)} %param.9) | copy-start | bytes 3076
  3.4 1.3 %copy-start.1 = (f32[256,1152]{1,0:T(8,128)S(1)}, f32[256,1152]{1,0:T(8,128)}, u32[]{:S(2)}) copy-start(f32[256,1152]{1,0:T(8,128)} %param.8) | copy-start | bytes 3538948
  5.1 74.3 %collective-permute-start.4 = (f32[256,1152]{1,0:T(8,128)S(1)}, f32[256,1152]{1,0:T(8,128)S(1)}, u32[]{:S(2)}, u32[]{:S(2)}) collective-permute-start(f32[256,1152]{1,0:T(8,128)S(1)} %convolution_add_fusion.1), channel_id=1, source_target_pairs={{767,0},{0,1},{1,2},{2,3},{3,4},{4,5},{5,6},{6,7},{7,8},{8,9},{9,1... | collective-permute-start | bytes 3538952 | tf_op jit(solution)/shard_map/ppermute | solution.py:12
  7.0 69.9 %collective-permute-start.1 = (bf16[256,1152]{1,0:T(8,128)(2,1)S(1)}, bf16[256,1152]{1,0:T(8,128)(2,1)S(1)}, u32[]{:S(2)}, u32[]{:S(2)}) collective-permute-start(bf16[256,1152]{1,0:T(8,128)(2,1)S(1)} %convert_element_type.15), channel_id=1, source_target_pairs={{767,0},{0,1},{1,2},{2,3},{3,4},{4,5},{5,6},{6,7},{7,8},{8,9},{9,1... | collective-permute-start | bytes 1769480 | tf_op jit(solution)/shard_map/ppermute | solution.py:12
  11.6 67.2 %collective-permute-start = (s32[256]{0:T(256)S(1)}, s32[256]{0:T(256)S(1)}, u32[]{:S(2)}, u32[]{:S(2)}) collective-permute-start(s32[256]{0:T(256)S(1)} %copy-done.2), channel_id=1, source_target_pairs={{767,0},{0,1},{1,2},{2,3},{3,4},{4,5},{5,6},{6,7},{7,8},{8,9},{9,1... | collective-permute-start | bytes 3080 | tf_op jit(solution)/shard_map/ppermute | solution.py:12
  76.9 36.2 %collective-permute-start.3 = (bf16[256,1152]{1,0:T(8,128)(2,1)S(1)}, bf16[256,1152]{1,0:T(8,128)(2,1)S(1)}, u32[]{:S(2)}, u32[]{:S(2)}) collective-permute-start(bf16[256,1152]{1,0:T(8,128)(2,1)S(1)} %collective-permute-done.1), channel_id=1, source_target_pairs={{767,0},{0,1},{1,2},{2,3},{3,4},{4,5},{5,6},{6,7},{7,8},{8,9},{9,1... | collective-permute-start | bytes 1769480 | tf_op jit(solution)/shard_map/ppermute | solution.py:12
  79.8 35.7 %collective-permute-start.5 = (f32[256,1152]{1,0:T(8,128)S(1)}, f32[256,1152]{1,0:T(8,128)S(1)}, u32[]{:S(2)}, u32[]{:S(2)}) collective-permute-start(f32[256,1152]{1,0:T(8,128)S(1)} %convolution_add_fusion), channel_id=1, source_target_pairs={{767,0},{0,1},{1,2},{2,3},{3,4},{4,5},{5,6},{6,7},{7,8},{8,9},{9,1... | collective-permute-start | bytes 3538952 | tf_op jit(solution)/shard_map/ppermute | solution.py:12
  82.2 30.9 %collective-permute-start.2 = (s32[256]{0:T(256)S(1)}, s32[256]{0:T(256)S(1)}, u32[]{:S(2)}, u32[]{:S(2)}) collective-permute-start(s32[256]{0:T(256)S(1)} %collective-permute-done), channel_id=1, source_target_pairs={{767,0},{0,1},{1,2},{2,3},{3,4},{4,5},{5,6},{6,7},{7,8},{8,9},{9,1... | collective-permute-start | bytes 3080 | tf_op jit(solution)/shard_map/ppermute | solution.py:12
where the time goes:
time: 117 us
  waiting for transfers between devices  91.9 us (79%)
  starting transfers between devices  14.2 us (12%)
  matrix products  6.02 us (5%)
  between operations  2.15 us (2%)
  other arithmetic  1.91 us (2%)
    ppermute x6, waiting for transfers between devices, from_behind(): return lax.ppermute(block, axis, route)  91.9 us
    ppermute x6, starting transfers between devices, from_behind(): return lax.ppermute(block, axis, route)  14.2 us
  transfers between devices with their start and end apart: 6, of which 2 were waited for; matrix products, arithmetic and copies ran while one was open for 4% of the time, Pallas kernels for 0%

commit v1 on v0

v1 whole, which is shorter than its diff:
```python
import functools

import jax
import jax.numpy as jnp
from jax import lax
from jax.experimental import pallas as pl
from jax.experimental.pallas import tpu as pltpu
from jax.sharding import PartitionSpec as P

SHIFTS = 2
Y = 8
TILE = 384
MESH = pl.DeviceIdType.MESH

AHEAD_T = [(64 + 32 * i, 32) for i in range(6)]
BACK_T = [(16 * i, 16) for i in range(4)]
AHEAD_C = [(64 + 32 * i, 32) for i in range(5)] + [(224, 16), (240, 16)]
BACK_C = [(16 * i, 16) for i in range(4)]


def places(zs, dps):
    dp = lax.axis_index("dp")
    group = lax.axis_index("group")
    core = group % 2
    y_hi = group // 2
    z = dp % zs
    y_lo = (dp // zs) % 2
    x = dp // (2 * zs)
    y = y_hi * 2 + y_lo

    def chip(x, y, z):
        return ((x * 2 + y % 2) * zs + z, (y // 2) * 2 + core)

    def after(place):
        dp, group = place
        return ((dp + group // 6) % dps, (group + 2) % 8)

    def before(place):
        dp, group = place
        return ((dp + dps - (7 - group) // 6) % dps, (group + 6) % 8)

    me = (dp, group)
    mate = (dp, group + 1 - 2 * core)
    via = chip(x, (y + Y - 3) % Y, z)
    source = chip(x, (y + 3) % Y, z)
    previous = before(me)
    p_dp, p_group = previous
    p_y = (p_group // 2) * 2 + (p_dp // zs) % 2
    p_via = chip(p_dp // (2 * zs), (p_y + Y - 3) % Y, p_dp % zs)
    return dict(
        core=core,
        mate=mate,
        after=after(me),
        previous=previous,
        via=via,
        source=source,
        onward=after(source),
        previous_via=p_via,
    )


def kernel(
    zs,
    dps,
    log_scale,
    bias,
    image_hbm,
    text_hbm,
    accum_hbm,
    ids_hbm,
    loss_hbm,
    image_grad_hbm,
    text_grad_hbm,
    image,
    text,
    accum,
    own,
    mate_text,
    far_text,
    coef,
    grad,
    part,
    mate_part,
    total,
    carried,
    far_carried,
    passing,
    loss,
    loss_row,
    image_grad,
    ids,
    mate_ids,
    far_ids,
    load_sem,
    store_sem,
    sends,
    recvs,
):
    at = places(zs, dps)
    core = at["core"]
    is0 = core == 0
    is1 = core == 1
    barrier = pltpu.get_barrier_semaphore()
    for name in ("mate", "previous", "source", "previous_via"):
        pl.semaphore_signal(barrier, inc=1, device_id=at[name], device_id_type=MESH)

    loads = [
        pltpu.make_async_copy(src, dst, load_sem.at[i])
        for i, (src, dst) in enumerate(
            [(text_hbm, text), (image_hbm, image), (ids_hbm, ids), (accum_hbm, accum)]
        )
    ]
    for copy in loads:
        copy.start()

    count = [0]

    def remote(src, dst, to):
        k = count[0]
        count[0] += 1
        return pltpu.make_async_remote_copy(
            src_ref=src,
            dst_ref=dst,
            send_sem=sends.at[k],
            recv_sem=recvs.at[k],
            device_id=at[to],
            device_id_type=MESH,
        )

    def rows(ref, piece, shift=0):
        return ref.at[pl.ds(piece[0] + shift, piece[1])]

    back_t = sum(n for _, n in BACK_T)
    text_ahead = [remote(rows(own, p), rows(far_text, p), "after") for p in AHEAD_T]
    text_leg1 = [remote(rows(own, p), rows(passing, p), "via") for p in BACK_T]
    text_leg2 = [remote(rows(passing, p), rows(far_text, p), "onward") for p in BACK_T]
    carry_ahead = [remote(rows(carried, p), rows(far_carried, p), "after") for p in AHEAD_C]
    carry_leg1 = [remote(rows(carried, p), rows(passing, p, back_t), "via") for p in BACK_C]
    carry_leg2 = [remote(rows(passing, p, back_t), rows(far_carried, p), "onward") for p in BACK_C]
    ids_ahead = remote(ids, far_ids, "after")
    text_down = remote(own, mate_text, "mate")
    ids_down = remote(ids, mate_ids, "mate")
    far_pieces = BACK_T + AHEAD_T
    text_up = [remote(rows(far_text, p), rows(mate_text, p), "mate") for p in far_pieces]
    ids_up = remote(far_ids, mate_ids, "mate")
    part_over = remote(part, mate_part, "mate")

    scale = jnp.exp(jnp.full((1, 256), log_scale[0], jnp.float32))
    shift = bias[0]

    def terms(text_block, text_ids, first, out):
        image_ids = jnp.transpose(jnp.broadcast_to(ids[...].astype(jnp.float32), (128, 256)))
        other = text_ids[...].astype(jnp.float32)
        for i in range(2):
            at_rows = pl.ds(128 * i, 128)
            logits = (
                scale
                * lax.dot_general(
                    image[at_rows, :],
                    text_block[...],
                    (((1,), (1,)), ((), ())),
                    preferred_element_type=jnp.float32,
                )
                + shift
            )
            mine = image_ids[128 * i : 128 * (i + 1), 0:1]
            minus = jnp.where(mine == other, -1.0, 1.0)
            u = minus * logits
            e = jnp.exp(-jnp.abs(u))
            soft = jnp.maximum(u, 0.0) + jnp.log1p(e)
            sig = jnp.where(u >= 0, 1.0, e) / (1.0 + e)
            coef[at_rows, :] = (minus * sig * scale).astype(jnp.bfloat16)
            folded = soft[:, :128] + soft[:, 128:]
            if first:
                loss[at_rows, :] = folded
            else:
                loss[at_rows, :] = loss[at_rows, :] + folded
        for j in range(image.shape[1] // TILE):
            cols = pl.ds(TILE * j, TILE)
            g = jnp.dot(coef[...], text_block[:, cols], preferred_element_type=jnp.float32)
            if first:
                grad[:, cols] = g
            else:
                grad[:, cols] = grad[:, cols] + g
            out[:, cols] = lax.dot_general(
                coef[...],
                image[:, cols],
                (((0,), (0,)), ((), ())),
                preferred_element_type=jnp.float32,
            )

    loads[0].wait()
    own[...] = text[...].astype(jnp.bfloat16)
    loads[1].wait()
    loads[2].wait()
    pl.semaphore_wait(barrier, 4)

    for i in range(max(len(text_leg1), len(text_ahead))):
        if i < len(text_leg1):
            text_leg1[i].start()
        if i < len(text_ahead):
            text_ahead[i].start()
        if i == 0:
            ids_ahead.start()

            @pl.when(is0)
            def _():
                text_down.start()
                ids_down.start()

    terms(own, ids, True, total)
    loads[3].wait()

    @pl.when(is1)
    def _():
        carried[...] = (total[...] + accum[...]).astype(jnp.bfloat16)
        text_down.wait_recv()
        ids_down.wait_recv()
        terms(mate_text, mate_ids, False, part)
        part_over.start()

    @pl.when(is0)
    def _():
        part_over.wait_recv()
        carried[...] = (total[...] + accum[...] + mate_part[...]).astype(jnp.bfloat16)

    for copy in carry_ahead:
        copy.start()
    for i in range(max(len(text_leg1), len(carry_leg1))):
        if i < len(text_leg1):
            text_leg1[i].wait_recv()
            text_leg2[i].start()
        if i < len(carry_leg1):
            carry_leg1[i].start()

    ids_ahead.wait_recv()

    @pl.when(is1)
    def _():
        ids_up.start()

    order = list(range(len(BACK_T), len(far_pieces))) + list(range(len(BACK_T)))
    for i in order:
        (text_leg2[i] if i < len(BACK_T) else text_ahead[i - len(BACK_T)]).wait_recv()

        @pl.when(is1)
        def _():
            text_up[i].start()

    @pl.when(is0)
    def _():
        ids_up.wait_recv()
        for i in order:
            text_up[i].wait_recv()
        terms(mate_text, mate_ids, False, part)
        part_over.start()

    terms(far_text, far_ids, False, total)

    image_grad[...] = grad[...].astype(jnp.bfloat16)
    store_image = pltpu.make_async_copy(image_grad, image_grad_hbm, store_sem.at[0])
    store_image.start()
    columns = (SHIFTS + 1) * image.shape[0]
    loss_row[...] = jnp.sum(jnp.transpose(loss[...]), axis=0, keepdims=True) / columns
    store_loss = pltpu.make_async_copy(loss_row, loss_hbm, store_sem.at[1])
    store_loss.start()

    @pl.when(is1)
    def _():
        part_over.wait_recv()
        total[...] = total[...] + mate_part[...]

    stores = []

    def finish(copy, piece):
        copy.wait_recv()
        at_rows = pl.ds(piece[0], piece[1])
        total[at_rows, :] = total[at_rows, :] + far_carried[at_rows, :].astype(jnp.float32)
        store = pltpu.make_async_copy(
            rows(total, piece), rows(text_grad_hbm, piece), store_sem.at[2 + len(stores)]
        )
        store.start()
        stores.append(store)

    half = len(carry_ahead) // 2
    for i in range(half):
        finish(carry_ahead[i], AHEAD_C[i])
    for i in range(len(carry_leg1)):
        carry_leg1[i].wait_recv()
        carry_leg2[i].start()
    for i in range(max(len(carry_ahead) - half, len(carry_leg2))):
        if half + i < len(carry_ahead):
            finish(carry_ahead[half + i], AHEAD_C[half + i])
        if i < len(carry_leg2):
            finish(carry_leg2[i], BACK_C[i])

    for group in (text_ahead, text_leg1, text_leg2, carry_ahead, carry_leg1, carry_leg2):
        for copy in group:
            copy.wait_send()
    ids_ahead.wait_send()
    part_over.wait_send()

    @pl.when(is0)
    def _():
        text_down.wait_send()
        ids_down.wait_send()

    @pl.when(is1)
    def _():
        ids_up.wait_send()
        for copy in text_up:
            copy.wait_send()

    store_image.wait()
    store_loss.wait()
    for store in stores:
        store.wait()


def solution(mesh):
    dps = mesh.shape["dp"]
    zs = dps // 8 if dps >= 8 else 1
    copies = 3 * len(BACK_T) + 2 * len(AHEAD_T) + len(AHEAD_C) + 2 * len(BACK_C) + 5
    pieces = len(AHEAD_C) + len(BACK_C)
    passing_rows = sum(n for _, n in BACK_T) + sum(n for _, n in BACK_C)

    def body(image_emb, text_emb, text_accum, pair_ids, log_scale, bias):
        n, d = image_emb.shape
        any_space = pl.BlockSpec(memory_space=pl.ANY)
        scalar = pl.BlockSpec(memory_space=pltpu.SMEM)
        f32, bf16, i32 = jnp.float32, jnp.bfloat16, jnp.int32
        loss, image_grad, text_grad = pl.pallas_call(
            functools.partial(kernel, zs, dps),
            out_shape=(
                jax.ShapeDtypeStruct((1, n), f32),
                jax.ShapeDtypeStruct((n, d), bf16),
                jax.ShapeDtypeStruct((n, d), f32),
            ),
            in_specs=[scalar, scalar, any_space, any_space, any_space, any_space],
            out_specs=(any_space, any_space, any_space),
            scratch_shapes=[
                pltpu.VMEM((n, d), bf16),
                pltpu.VMEM((n, d), f32),
                pltpu.VMEM((n, d), f32),
                pltpu.VMEM((n, d), bf16),
                pltpu.VMEM((n, d), bf16),
                pltpu.VMEM((n, d), bf16),
                pltpu.VMEM((n, n), bf16),
                pltpu.VMEM((n, d), f32),
                pltpu.VMEM((n, d), f32),
                pltpu.VMEM((n, d), f32),
                pltpu.VMEM((n, d), f32),
                pltpu.VMEM((n, d), bf16),
                pltpu.VMEM((n, d), bf16),
                pltpu.VMEM((passing_rows, d), bf16),
                pltpu.VMEM((n, 128), f32),
                pltpu.VMEM((1, n), f32),
                pltpu.VMEM((n, d), bf16),
                pltpu.VMEM((1, n), i32),
                pltpu.VMEM((1, n), i32),
                pltpu.VMEM((1, n), i32),
                pltpu.SemaphoreType.DMA((4,)),
                pltpu.SemaphoreType.DMA((2 + pieces,)),
                pltpu.SemaphoreType.DMA((copies,)),
                pltpu.SemaphoreType.DMA((copies,)),
            ],
            compiler_params=pltpu.CompilerParams(
                collective_id=0, has_side_effects=True, vmem_limit_bytes=40 << 20
            ),
        )(log_scale, bias, image_emb, text_emb, text_accum, pair_ids.reshape(1, n))
        return loss.reshape(n), image_grad, text_grad

    split = P(("dp", "group"))
    wide = P(("dp", "group"), None)
    return jax.shard_map(
        body,
        mesh=mesh,
        in_specs=(wide, wide, wide, split, P(), P()),
        out_specs=(split, wide, wide),
        check_vma=False,
    )
```

time: 117 us -> 81.8 us (0.70)
  the two profiles are of different devices: /device:TPU:62 before, /device:TPU:38 now
where the time goes in v1:
time: 81.8 us; the launch traced here: 81.5 us
  Pallas kernels  72.9 us (89%)
  local copies, waits for them, and re-layouts  6.67 us (8%)
  between operations  1.94 us (2%)
    pallas_call x1, Pallas kernels, body(): pl.pallas_call(functools.partial(kernel, zs, dps), out_shape=(jax.ShapeDt...  72.9 us
    unnamed x11, local copies, waits for them, and re-layouts  6.67 us

profile of v1, /device:TPU:38, one launch (start us, length us, event | category | flops | bytes accessed | tf_op | source)
XLA Modules:
  0.0 81.5 jit_solution(17730787856383381500)
XLA Ops:
  1.9 0.0 copy-start
  1.9 1.3 %copy-done = f32[256,1152]{1,0:T(8,128)S(1)} copy-done((f32[256,1152]{1,0:T(8,128)S(1)}, f32[256,1152]{1,0:T(8,128)}, u32[]{:S(2)}) %copy-start) | copy-done | bytes 1179672
  3.2 0.0 copy-start.1
  3.2 1.3 %copy-done.1 = f32[256,1152]{1,0:T(8,128)S(1)} copy-done((f32[256,1152]{1,0:T(8,128)S(1)}, f32[256,1152]{1,0:T(8,128)}, u32[]{:S(2)}) %copy-start.1) | copy-done | bytes 1179672
  4.5 0.0 copy-start.2
  4.5 1.1 %copy-done.2 = bf16[256,1152]{1,0:T(8,128)(2,1)S(1)} copy-done((bf16[256,1152]{1,0:T(8,128)(2,1)S(1)}, bf16[256,1152]{1,0:T(8,128)(2,1)}, u32[]{:S(2)}) %copy-start.2) | copy-done | bytes 589848
  5.5 0.0 copy-start.3
  5.5 0.7 copy-done.3
  6.2 72.9 %shard_map.85 = (f32[1,256]{1,0:T(1,128)S(1)}, bf16[256,1152]{1,0:T(8,128)(2,1)S(1)}, f32[256,1152]{1,0:T(8,128)S(1)}) custom-call(f32[1]{0:T(128)S(6)} %copy.12.log_scale, f32[1]{0:T(128)S(6)} %copy.13.bias, bf16[256,1152]{1,0:T(8,128)(2,1)S(1)} %copy-done.2, f32[256,1152]{1,0:T(8,128)S(1)} %copy-done, f32[256,1152]{1,0:T(8,128)S(1)} %copy-done.1, ...), custom_call_target="tpu_custom_call" | custom-call | tf_op jit(solution)/shard_map/pallas_call | solution.py:332
  79.1 0.6 copy.14
  79.7 0.8 copy.15
  80.5 1.0 %copy.16 = f32[256,1152]{1,0:T(8,128)} copy(f32[256,1152]{1,0:T(8,128)S(1)} %get-tuple-element.14) | data formatting | bytes 2359296
Async XLA Ops:
  1.9 1.3 %copy-start = (f32[256,1152]{1,0:T(8,128)S(1)}, f32[256,1152]{1,0:T(8,128)}, u32[]{:S(2)}) copy-start(f32[256,1152]{1,0:T(8,128)} %text_hbm.1) | copy-start | bytes 3538948
  3.2 1.3 %copy-start.1 = (f32[256,1152]{1,0:T(8,128)S(1)}, f32[256,1152]{1,0:T(8,128)}, u32[]{:S(2)}) copy-start(f32[256,1152]{1,0:T(8,128)} %accum_hbm.1) | copy-start | bytes 3538948
  4.5 1.1 %copy-start.2 = (bf16[256,1152]{1,0:T(8,128)(2,1)S(1)}, bf16[256,1152]{1,0:T(8,128)(2,1)}, u32[]{:S(2)}) copy-start(bf16[256,1152]{1,0:T(8,128)(2,1)} %image_hbm.1) | copy-start | bytes 1769476
  5.5 0.7 copy-start.3

commit v2 on v1

--- a/solution.py
+++ b/solution.py
@@ -16,6 +16,8 @@
 BACK_T = [(16 * i, 16) for i in range(4)]
 AHEAD_C = [(64 + 32 * i, 32) for i in range(5)] + [(224, 16), (240, 16)]
 BACK_C = [(16 * i, 16) for i in range(4)]
+SWING_T = [2, 3]
+SWING_C = [2, 3]
 
 
 def places(zs, dps):
@@ -47,8 +49,13 @@
     p_dp, p_group = previous
     p_y = (p_group // 2) * 2 + (p_dp // zs) % 2
     p_via = chip(p_dp // (2 * zs), (p_y + Y - 3) % Y, p_dp % zs)
+    last = z == zs - 1
     return dict(
         core=core,
+        long=last & (y == 6),
+        long_relay=last & (y == 3),
+        short=last & (y == 7),
+        short_relay=last & (y == 4),
         mate=mate,
         after=after(me),
         previous=previous,
@@ -62,8 +69,8 @@
 def kernel(
     zs,
     dps,
-    log_scale,
-    bias,
+    log_scale_hbm,
+    bias_hbm,
     image_hbm,
     text_hbm,
     accum_hbm,
@@ -91,6 +98,8 @@
     ids,
     mate_ids,
     far_ids,
+    log_scale,
+    bias,
     load_sem,
     store_sem,
     sends,
@@ -107,7 +116,14 @@
     loads = [
         pltpu.make_async_copy(src, dst, load_sem.at[i])
         for i, (src, dst) in enumerate(
-            [(text_hbm, text), (image_hbm, image), (ids_hbm, ids), (accum_hbm, accum)]
+            [
+                (text_hbm, text),
+                (image_hbm, image),
+                (ids_hbm, ids),
+                (log_scale_hbm, log_scale),
+                (bias_hbm, bias),
+                (accum_hbm, accum),
+            ]
         )
     ]
     for copy in loads:
@@ -115,14 +131,17 @@
 
     count = [0]
 
-    def remote(src, dst, to):
-        k = count[0]
+    def fresh():
         count[0] += 1
+        return count[0] - 1
+
+    def remote(src, dst, to, send=None, recv=None):
+        k = fresh() if send is None or recv is None else 0
         return pltpu.make_async_remote_copy(
             src_ref=src,
             dst_ref=dst,
-            send_sem=sends.at[k],
-            recv_sem=recvs.at[k],
+            send_sem=sends.at[k if send is None else send],
+            recv_sem=recvs.at[k if recv is None else recv],
             device_id=at[to],
             device_id_type=MESH,
         )
@@ -130,25 +149,114 @@
     def rows(ref, piece, shift=0):
         return ref.at[pl.ds(piece[0] + shift, piece[1])]
 
-    back_t = sum(n for _, n in BACK_T)
-    text_ahead = [remote(rows(own, p), rows(far_text, p), "after") for p in AHEAD_T]
-    text_leg1 = [remote(rows(own, p), rows(passing, p), "via") for p in BACK_T]
-    text_leg2 = [remote(rows(passing, p), rows(far_text, p), "onward") for p in BACK_T]
-    carry_ahead = [remote(rows(carried, p), rows(far_carried, p), "after") for p in AHEAD_C]
-    carry_leg1 = [remote(rows(carried, p), rows(passing, p, back_t), "via") for p in BACK_C]
-    carry_leg2 = [remote(rows(passing, p, back_t), rows(far_carried, p), "onward") for p in BACK_C]
+    short, short_relay = at["short"], at["short_relay"]
+    long, long_relay = at["long"], at["long_relay"]
+    room = [0]
+
+    class Stream:
+        def __init__(self, src, dst, ahead, back, swing):
+            self.ahead, self.back, self.swing = ahead, back, swing
+            ahead_ids = [fresh() for _ in ahead]
+            leg1_ids = [fresh() for _ in back]
+            leg2_ids = [fresh() for _ in back]
+            swing_ids = [fresh() for _ in swing]
+
+            def hop(src, dst, to, send, recv):
+                return remote(src, dst, to, send, recv)
+
+            def slot(piece):
+                room[0] += piece[1]
+                return passing.at[pl.ds(room[0] - piece[1], piece[1])]
+
+            slots = [slot(p) for p in back]
+            swing_slots = [slot(ahead[i]) for i in swing]
+            self.straight = [
+                hop(rows(src, p), rows(dst, p), "after", k, k) for p, k in zip(ahead, ahead_ids)
+            ]
+            self.leg1 = [
+                hop(rows(src, p), t, "via", k, k) for p, t, k in zip(back, slots, leg1_ids)
+            ]
+            self.leg2 = [
+                hop(t, rows(dst, p), "onward", k, k) for p, t, k in zip(back, slots, leg2_ids)
+            ]
+            self.instead = [
+                hop(rows(src, p), rows(dst, p), "after", k1, k2)
+                for p, k1, k2 in zip(back, leg1_ids, leg2_ids)
+            ]
+            self.swing1 = [
+                hop(rows(src, ahead[i]), t, "via", ahead_ids[i], k)
+                for i, t, k in zip(swing, swing_slots, swing_ids)
+            ]
+            self.swing2 = [
+                hop(t, rows(dst, ahead[i]), "onward", k, ahead_ids[i])
+                for i, t, k in zip(swing, swing_slots, swing_ids)
+            ]
+
+        def send_ahead(self, i):
+            if i in self.swing:
+
+                @pl.when(long)
+                def _():
+                    self.swing1[self.swing.index(i)].start()
+
+                @pl.when(jnp.logical_not(long))
+                def _():
+                    self.straight[i].start()
+
+            else:
+                self.straight[i].start()
+
+        def send_back(self, i):
+            @pl.when(short)
+            def _():
+                self.instead[i].start()
+
+            @pl.when(jnp.logical_not(short))
+            def _():
+                self.leg1[i].start()
+
+        def relay(self, i):
+            @pl.when(jnp.logical_not(short_relay))
+            def _():
+                self.leg1[i].wait_recv()
+                self.leg2[i].start()
+
+        def relay_swing(self):
+            @pl.when(long_relay)
+            def _():
+                for one, two in zip(self.swing1, self.swing2):
+                    one.wait_recv()
+                    two.start()
+
+        def wait_sends(self):
+            for copy in self.straight + self.leg1:
+                copy.wait_send()
+
+            @pl.when(jnp.logical_not(short_relay))
+            def _():
+                for copy in self.leg2:
+                    copy.wait_send()
+
+            @pl.when(long_relay)
+            def _():
+                for copy in self.swing2:
+                    copy.wait_send()
+
+    texts = Stream(own, far_text, AHEAD_T, BACK_T, SWING_T)
+    carries = Stream(carried, far_carried, AHEAD_C, BACK_C, SWING_C)
     ids_ahead = remote(ids, far_ids, "after")
     text_down = remote(own, mate_text, "mate")
     ids_down = remote(ids, mate_ids, "mate")
-    far_pieces = BACK_T + AHEAD_T
-    text_up = [remote(rows(far_text, p), rows(mate_text, p), "mate") for p in far_pieces]
+    arrivals = [(texts.straight[i], AHEAD_T[i]) for i in range(len(AHEAD_T)) if i not in SWING_T]
+    arrivals += [(texts.leg2[i], BACK_T[i]) for i in range(len(BACK_T))]
+    arrivals += [(texts.straight[i], AHEAD_T[i]) for i in SWING_T]
+    text_up = [remote(rows(far_text, p), rows(mate_text, p), "mate") for _, p in arrivals]
     ids_up = remote(far_ids, mate_ids, "mate")
     part_over = remote(part, mate_part, "mate")
 
-    scale = jnp.exp(jnp.full((1, 256), log_scale[0], jnp.float32))
-    shift = bias[0]
-
     def terms(text_block, text_ids, first, out):
+        scale = jnp.exp(jnp.full((1, 256), log_scale[0], jnp.float32))
+        shift = bias[0]
         image_ids = jnp.transpose(jnp.broadcast_to(ids[...].astype(jnp.float32), (128, 256)))
         other = text_ids[...].astype(jnp.float32)
         for i in range(2):
@@ -191,15 +299,22 @@
 
     loads[0].wait()
     own[...] = text[...].astype(jnp.bfloat16)
-    loads[1].wait()
-    loads[2].wait()
+    for copy in loads[1:5]:
+        copy.wait()
+    terms(own, ids, True, total)
+    loads[5].wait()
+
+    @pl.when(is1)
+    def _():
+        carried[...] = (total[...] + accum[...]).astype(jnp.bfloat16)
+
     pl.semaphore_wait(barrier, 4)
 
-    for i in range(max(len(text_leg1), len(text_ahead))):
-        if i < len(text_leg1):
-            text_leg1[i].start()
-        if i < len(text_ahead):
-            text_ahead[i].start()
+    for i in range(max(len(BACK_T), len(AHEAD_T))):
+        if i < len(BACK_T):
+            texts.send_back(i)
+        if i < len(AHEAD_T):
+            texts.send_ahead(i)
         if i == 0:
             ids_ahead.start()
 
@@ -208,12 +323,8 @@
                 text_down.start()
                 ids_down.start()
 
-    terms(own, ids, True, total)
-    loads[3].wait()
-
     @pl.when(is1)
     def _():
-        carried[...] = (total[...] + accum[...]).astype(jnp.bfloat16)
         text_down.wait_recv()
         ids_down.wait_recv()
         terms(mate_text, mate_ids, False, part)
@@ -224,14 +335,14 @@
         part_over.wait_recv()
         carried[...] = (total[...] + accum[...] + mate_part[...]).astype(jnp.bfloat16)
 
-    for copy in carry_ahead:
-        copy.start()
-    for i in range(max(len(text_leg1), len(carry_leg1))):
-        if i < len(text_leg1):
-            text_leg1[i].wait_recv()
-            text_leg2[i].start()
-        if i < len(carry_leg1):
-            carry_leg1[i].start()
+    for i in range(len(AHEAD_C)):
+        carries.send_ahead(i)
+    for i in range(max(len(BACK_T), len(BACK_C))):
+        if i < len(BACK_T):
+            texts.relay(i)
+        if i < len(BACK_C):
+            carries.send_back(i)
+    texts.relay_swing()
 
     ids_ahead.wait_recv()
 
@@ -239,21 +350,28 @@
     def _():
         ids_up.start()
 
-    order = list(range(len(BACK_T), len(far_pieces))) + list(range(len(BACK_T)))
-    for i in order:
-        (text_leg2[i] if i < len(BACK_T) else text_ahead[i - len(BACK_T)]).wait_recv()
+    for i, (copy, _) in enumerate(arrivals):
+        copy.wait_recv()
 
         @pl.when(is1)
         def _():
             text_up[i].start()
 
+    early = len(BACK_C) // 2
+    for i in range(early):
+        carries.relay(i)
+
     @pl.when(is0)
     def _():
         ids_up.wait_recv()
-        for i in order:
-            text_up[i].wait_recv()
+        for copy in text_up:
+            copy.wait_recv()
         terms(mate_text, mate_ids, False, part)
         part_over.start()
+
+    for i in range(early, len(BACK_C)):
+        carries.relay(i)
+    carries.relay_swing()
 
     terms(far_text, far_ids, False, total)
 
@@ -282,21 +400,15 @@
         store.start()
         stores.append(store)
 
-    half = len(carry_ahead) // 2
+    half = len(AHEAD_C) - len(BACK_C)
     for i in range(half):
-        finish(carry_ahead[i], AHEAD_C[i])
-    for i in range(len(carry_leg1)):
-        carry_leg1[i].wait_recv()
-        carry_leg2[i].start()
-    for i in range(max(len(carry_ahead) - half, len(carry_leg2))):
-        if half + i < len(carry_ahead):
-            finish(carry_ahead[half + i], AHEAD_C[half + i])
-        if i < len(carry_leg2):
-            finish(carry_leg2[i], BACK_C[i])
-
-    for group in (text_ahead, text_leg1, text_leg2, carry_ahead, carry_leg1, carry_leg2):
-        for copy in group:
-            copy.wait_send()
+        finish(carries.straight[i], AHEAD_C[i])
+    for i in range(len(BACK_C)):
+        finish(carries.leg2[i], BACK_C[i])
+        finish(carries.straight[half + i], AHEAD_C[half + i])
+
+    texts.wait_sends()
+    carries.wait_sends()
     ids_ahead.wait_send()
     part_over.wait_send()
 
@@ -317,26 +429,42 @@
         store.wait()
 
 
+def store_kernel(loss, image_grad, text_grad, loss_hbm, image_grad_hbm, text_grad_hbm, sem):
+    copies = [
+        pltpu.make_async_copy(src, dst, sem.at[i])
+        for i, (src, dst) in enumerate(
+            [(text_grad, text_grad_hbm), (image_grad, image_grad_hbm), (loss, loss_hbm)]
+        )
+    ]
+    for copy in copies:
+        copy.start()
+    for copy in copies:
+        copy.wait()
+
+
 def solution(mesh):
     dps = mesh.shape["dp"]
     zs = dps // 8 if dps >= 8 else 1
     copies = 3 * len(BACK_T) + 2 * len(AHEAD_T) + len(AHEAD_C) + 2 * len(BACK_C) + 5
+    copies += len(SWING_T) + len(SWING_C)
     pieces = len(AHEAD_C) + len(BACK_C)
     passing_rows = sum(n for _, n in BACK_T) + sum(n for _, n in BACK_C)
+    passing_rows += sum(AHEAD_T[i][1] for i in SWING_T) + sum(AHEAD_C[i][1] for i in SWING_C)
 
     def body(image_emb, text_emb, text_accum, pair_ids, log_scale, bias):
         n, d = image_emb.shape
         any_space = pl.BlockSpec(memory_space=pl.ANY)
-        scalar = pl.BlockSpec(memory_space=pltpu.SMEM)
+        hbm = pl.BlockSpec(memory_space=pltpu.HBM)
         f32, bf16, i32 = jnp.float32, jnp.bfloat16, jnp.int32
-        loss, image_grad, text_grad = pl.pallas_call(
+        shapes = (
+            jax.ShapeDtypeStruct((1, n), f32),
+            jax.ShapeDtypeStruct((n, d), bf16),
+            jax.ShapeDtypeStruct((n, d), f32),
+        )
+        results = pl.pallas_call(
             functools.partial(kernel, zs, dps),
-            out_shape=(
-                jax.ShapeDtypeStruct((1, n), f32),
-                jax.ShapeDtypeStruct((n, d), bf16),
-                jax.ShapeDtypeStruct((n, d), f32),
-            ),
-            in_specs=[scalar, scalar, any_space, any_space, any_space, any_space],
+            out_shape=shapes,
+            in_specs=[hbm] * 6,
             out_specs=(any_space, any_space, any_space),
             scratch_shapes=[
                 pltpu.VMEM((n, d), bf16),
@@ -359,15 +487,25 @@
                 pltpu.VMEM((1, n), i32),
                 pltpu.VMEM((1, n), i32),
                 pltpu.VMEM((1, n), i32),
-                pltpu.SemaphoreType.DMA((4,)),
+                pltpu.SMEM((1,), f32),
+                pltpu.SMEM((1,), f32),
+                pltpu.SemaphoreType.DMA((6,)),
                 pltpu.SemaphoreType.DMA((2 + pieces,)),
                 pltpu.SemaphoreType.DMA((copies,)),
                 pltpu.SemaphoreType.DMA((copies,)),
             ],
             compiler_params=pltpu.CompilerParams(
-                collective_id=0, has_side_effects=True, vmem_limit_bytes=40 << 20
+                collective_id=0, has_side_effects=True, vmem_limit_bytes=51 << 20
             ),
         )(log_scale, bias, image_emb, text_emb, text_accum, pair_ids.reshape(1, n))
+        loss, image_grad, text_grad = pl.pallas_call(
+            store_kernel,
+            out_shape=shapes,
+            in_specs=[any_space] * 3,
+            out_specs=(hbm, hbm, hbm),
+            scratch_shapes=[pltpu.SemaphoreType.DMA((3,))],
+            compiler_params=pltpu.CompilerParams(vmem_limit_bytes=1 << 20),
+        )(*results)
         return loss.reshape(n), image_grad, text_grad
 
     split = P(("dp", "group"))

time: 81.8 us -> 72.3 us (0.88)
  the two profiles are of different devices: /device:TPU:38 before, /device:TPU:10 now
where the time goes in v2:
time: 72.3 us; the launch traced here: 72.1 us
  Pallas kernels  68.4 us (95%)
  between operations  1.94 us (3%)
  local copies, waits for them, and re-layouts  1.74 us (2%)
    pallas_call x1, Pallas kernels, body(): pl.pallas_call(functools.partial(kernel, zs, dps), out_shape=shapes, in_s...  67.2 us
    unnamed x4, local copies, waits for them, and re-layouts  1.74 us

profile of v2, /device:TPU:10, one launch (start us, length us, event | category | flops | bytes accessed | tf_op | source)
XLA Modules:
  0.0 72.1 jit_solution(8279187814494821586)
XLA Ops:
  1.9 0.0 copy-start
  1.9 1.1 %copy-done = bf16[256,1152]{1,0:T(8,128)(2,1)S(1)} copy-done((bf16[256,1152]{1,0:T(8,128)(2,1)S(1)}, bf16[256,1152]{1,0:T(8,128)(2,1)}, u32[]{:S(2)}) %copy-start) | copy-done | bytes 589848
  3.0 0.0 copy-start.1
  3.0 0.7 copy-done.1
  3.7 67.2 %shard_map.85 = (f32[1,256]{1,0:T(1,128)S(1)}, bf16[256,1152]{1,0:T(8,128)(2,1)S(1)}, f32[256,1152]{1,0:T(8,128)S(1)}) custom-call(f32[1]{0:T(128)S(6)} %copy.9.log_scale_hbm, f32[1]{0:T(128)S(6)} %copy.10.bias_hbm, bf16[256,1152]{1,0:T(8,128)(2,1)S(1)} %copy-done, f32[256,1152]{1,0:T(8,128)} %text_hbm.1, f32[256,1152]{1,0:T(8,128)} %accum_hbm.1, ...), custom_call_target="tpu_custom_call" | custom-call | tf_op jit(solution)/shard_map/pallas_call | solution.py:464
  70.9 1.2 %shard_map.86 = (f32[1,256]{1,0:T(1,128)}, bf16[256,1152]{1,0:T(8,128)(2,1)}, f32[256,1152]{1,0:T(8,128)}) custom-call(f32[1,256]{1,0:T(1,128)S(1)} %get-tuple-element.9.loss, bf16[256,1152]{1,0:T(8,128)(2,1)S(1)} %get-tuple-element.10.image_grad, f32[256,1152]{1,0:T(8,128)S(1)} %get-tuple-element.11.text_grad), custom_call_target="tpu_custom_call" | custom-call | tf_op jit(solution)/shard_map/pallas_call | solution.py:501
Async XLA Ops:
  1.9 1.1 %copy-start = (bf16[256,1152]{1,0:T(8,128)(2,1)S(1)}, bf16[256,1152]{1,0:T(8,128)(2,1)}, u32[]{:S(2)}) copy-start(bf16[256,1152]{1,0:T(8,128)(2,1)} %image_hbm.1) | copy-start | bytes 1769476
  3.0 0.7 copy-start.1

commit v3 on v2

--- a/solution.py
+++ b/solution.py
@@ -16,19 +16,20 @@
 BACK_T = [(16 * i, 16) for i in range(4)]
 AHEAD_C = [(64 + 32 * i, 32) for i in range(5)] + [(224, 16), (240, 16)]
 BACK_C = [(16 * i, 16) for i in range(4)]
-SWING_T = [2, 3]
-SWING_C = [2, 3]
+HELP_T = {12: (1, 2, 3, 4, 5, 6, 7, 8, 9, 10)}
+HELP_C = {12: (1, 2, 3, 4)}
 
 
 def places(zs, dps):
     dp = lax.axis_index("dp")
     group = lax.axis_index("group")
+    xs = max(dps // (2 * zs), 1)
     core = group % 2
-    y_hi = group // 2
     z = dp % zs
-    y_lo = (dp // zs) % 2
+    y = (group // 2) * 2 + (dp // zs) % 2
     x = dp // (2 * zs)
-    y = y_hi * 2 + y_lo
+    last = z == zs - 1
+    helpers = HELP_T.get(zs, ())
 
     def chip(x, y, z):
         return ((x * 2 + y % 2) * zs + z, (y // 2) * 2 + core)
@@ -37,32 +38,37 @@
         dp, group = place
         return ((dp + group // 6) % dps, (group + 2) % 8)
 
-    def before(place):
-        dp, group = place
-        return ((dp + dps - (7 - group) // 6) % dps, (group + 6) % 8)
-
-    me = (dp, group)
-    mate = (dp, group + 1 - 2 * core)
-    via = chip(x, (y + Y - 3) % Y, z)
-    source = chip(x, (y + 3) % Y, z)
-    previous = before(me)
+    def relay(x, y, z):
+        turn = jnp.where((z == zs - 1) & (y == 6), 1, 0)
+        return chip(x, (y + Y - 3 + turn) % Y, z)
+
+    source = chip(x, (y + 3 - jnp.where(last & (y == 4), 1, 0)) % Y, z)
+    previous = ((dp + dps - (7 - group) // 6) % dps, (group + 6) % 8)
     p_dp, p_group = previous
+    p_z = p_dp % zs
     p_y = (p_group // 2) * 2 + (p_dp // zs) % 2
-    p_via = chip(p_dp // (2 * zs), (p_y + Y - 3) % Y, p_dp % zs)
-    last = z == zs - 1
+    helper = z < 0
+    for z_j in helpers:
+        helper = helper | ((y == 0) & (z == z_j))
     return dict(
         core=core,
-        long=last & (y == 6),
-        long_relay=last & (y == 3),
+        z=z,
         short=last & (y == 7),
-        short_relay=last & (y == 4),
-        mate=mate,
-        after=after(me),
+        idle=last & (y == 3),
+        end=(p_z == zs - 1) & (p_y == 7),
+        late=(p_z == zs - 1) & (p_y >= 6),
+        helper=helper,
+        mate=(dp, group + 1 - 2 * core),
+        after=after((dp, group)),
         previous=previous,
-        via=via,
+        via=relay(x, y, z),
         source=source,
         onward=after(source),
-        previous_via=p_via,
+        previous_via=relay(p_dp // (2 * zs), p_y, p_z),
+        helped=chip(x, 7, zs - 1),
+        help_end=chip((x + 1) % xs, 0, 0),
+        helpers=[chip(x, 0, z_j) for z_j in helpers],
+        end_helpers=[chip((x + xs - 1) % xs, 0, z_j) for z_j in helpers],
     )
 
 
@@ -109,9 +115,36 @@
     core = at["core"]
     is0 = core == 0
     is1 = core == 1
+    short, idle, end, helper = at["short"], at["idle"], at["end"], at["helper"]
+    helpers = HELP_T.get(zs, ())
     barrier = pltpu.get_barrier_semaphore()
-    for name in ("mate", "previous", "source", "previous_via"):
-        pl.semaphore_signal(barrier, inc=1, device_id=at[name], device_id_type=MESH)
+
+    def greet(place):
+        pl.semaphore_signal(barrier, inc=1, device_id=place, device_id_type=MESH)
+
+    greet(at["mate"])
+    greet(at["previous"])
+
+    @pl.when(jnp.logical_not(idle))
+    def _():
+        greet(at["source"])
+
+    @pl.when(jnp.logical_not(end))
+    def _():
+        greet(at["previous_via"])
+
+    if helpers:
+
+        @pl.when(end)
+        def _():
+            for place in at["end_helpers"]:
+                greet(place)
+
+        @pl.when(helper)
+        def _():
+            greet(at["helped"])
+
+    partners = 2 + jnp.where(short, len(helpers), 1) + jnp.where(idle, 0, 1) + jnp.where(helper, 1, 0)
 
     loads = [
         pltpu.make_async_copy(src, dst, load_sem.at[i])
@@ -142,64 +175,58 @@
             dst_ref=dst,
             send_sem=sends.at[k if send is None else send],
             recv_sem=recvs.at[k if recv is None else recv],
-            device_id=at[to],
+            device_id=at[to] if isinstance(to, str) else to,
             device_id_type=MESH,
         )
 
     def rows(ref, piece, shift=0):
         return ref.at[pl.ds(piece[0] + shift, piece[1])]
 
-    short, short_relay = at["short"], at["short_relay"]
-    long, long_relay = at["long"], at["long_relay"]
     room = [0]
 
+    def slot(n):
+        room[0] += n
+        return passing.at[pl.ds(room[0] - n, n)]
+
     class Stream:
-        def __init__(self, src, dst, ahead, back, swing):
-            self.ahead, self.back, self.swing = ahead, back, swing
+        def __init__(self, src, dst, ahead, back, help_z):
+            self.ahead, self.back = ahead, back
             ahead_ids = [fresh() for _ in ahead]
             leg1_ids = [fresh() for _ in back]
             leg2_ids = [fresh() for _ in back]
-            swing_ids = [fresh() for _ in swing]
-
-            def hop(src, dst, to, send, recv):
-                return remote(src, dst, to, send, recv)
-
-            def slot(piece):
-                room[0] += piece[1]
-                return passing.at[pl.ds(room[0] - piece[1], piece[1])]
-
-            slots = [slot(p) for p in back]
-            swing_slots = [slot(ahead[i]) for i in swing]
             self.straight = [
-                hop(rows(src, p), rows(dst, p), "after", k, k) for p, k in zip(ahead, ahead_ids)
+                remote(rows(src, p), rows(dst, p), "after", k, k) for p, k in zip(ahead, ahead_ids)
             ]
+            slots = [slot(n) for _, n in back]
             self.leg1 = [
-                hop(rows(src, p), t, "via", k, k) for p, t, k in zip(back, slots, leg1_ids)
+                remote(rows(src, p), t, "via", k, k) for p, t, k in zip(back, slots, leg1_ids)
             ]
             self.leg2 = [
-                hop(t, rows(dst, p), "onward", k, k) for p, t, k in zip(back, slots, leg2_ids)
+                remote(t, rows(dst, p), "onward", k, k) for p, t, k in zip(back, slots, leg2_ids)
             ]
             self.instead = [
-                hop(rows(src, p), rows(dst, p), "after", k1, k2)
+                remote(rows(src, p), rows(dst, p), "after", k1, k2)
                 for p, k1, k2 in zip(back, leg1_ids, leg2_ids)
             ]
-            self.swing1 = [
-                hop(rows(src, ahead[i]), t, "via", ahead_ids[i], k)
-                for i, t, k in zip(swing, swing_slots, swing_ids)
-            ]
-            self.swing2 = [
-                hop(t, rows(dst, ahead[i]), "onward", k, ahead_ids[i])
-                for i, t, k in zip(swing, swing_slots, swing_ids)
-            ]
+            self.help1, self.help2, self.help_z = [], [], help_z
+            if help_z:
+                marks = list(zip(back, leg1_ids, leg2_ids)) + list(zip(ahead, ahead_ids, ahead_ids))
+                marks = marks[: len(help_z)]
+                k, spot = fresh(), room[0]
+                slot(max(p[1] for p, _, _ in marks))
+                for j, (p, k1, k2) in enumerate(marks):
+                    here = passing.at[pl.ds(spot, p[1])]
+                    self.help1.append(remote(rows(src, p), here, at["helpers"][j], k1, k))
+                    self.help2.append(remote(here, rows(dst, p), "help_end", k, k2))
 
         def send_ahead(self, i):
-            if i in self.swing:
-
-                @pl.when(long)
+            if len(self.back) + i < len(self.help1):
+
+                @pl.when(short)
                 def _():
-                    self.swing1[self.swing.index(i)].start()
-
-                @pl.when(jnp.logical_not(long))
+                    self.help1[len(self.back) + i].start()
+
+                @pl.when(jnp.logical_not(short))
                 def _():
                     self.straight[i].start()
 
@@ -209,47 +236,49 @@
         def send_back(self, i):
             @pl.when(short)
             def _():
-                self.instead[i].start()
+                (self.help1 if self.help1 else self.instead)[i].start()
 
             @pl.when(jnp.logical_not(short))
             def _():
                 self.leg1[i].start()
 
         def relay(self, i):
-            @pl.when(jnp.logical_not(short_relay))
+            @pl.when(jnp.logical_not(idle))
             def _():
                 self.leg1[i].wait_recv()
                 self.leg2[i].start()
 
-        def relay_swing(self):
-            @pl.when(long_relay)
-            def _():
-                for one, two in zip(self.swing1, self.swing2):
-                    one.wait_recv()
-                    two.start()
+        def each_helper(self, act):
+            for z_j, one, two in zip(self.help_z, self.help1, self.help2):
+
+                @pl.when(helper & (at["z"] == z_j))
+                def _():
+                    act(one, two)
+
+        def help(self):
+            def act(one, two):
+                one.wait_recv()
+                two.start()
+
+            self.each_helper(act)
 
         def wait_sends(self):
             for copy in self.straight + self.leg1:
                 copy.wait_send()
 
-            @pl.when(jnp.logical_not(short_relay))
+            @pl.when(jnp.logical_not(idle))
             def _():
                 for copy in self.leg2:
                     copy.wait_send()
 
-            @pl.when(long_relay)
-            def _():
-                for copy in self.swing2:
-                    copy.wait_send()
-
-    texts = Stream(own, far_text, AHEAD_T, BACK_T, SWING_T)
-    carries = Stream(carried, far_carried, AHEAD_C, BACK_C, SWING_C)
+            self.each_helper(lambda one, two: two.wait_send())
+
+    texts = Stream(own, far_text, AHEAD_T, BACK_T, HELP_T.get(zs, ()))
+    carries = Stream(carried, far_carried, AHEAD_C, BACK_C, HELP_C.get(zs, ()))
     ids_ahead = remote(ids, far_ids, "after")
     text_down = remote(own, mate_text, "mate")
     ids_down = remote(ids, mate_ids, "mate")
-    arrivals = [(texts.straight[i], AHEAD_T[i]) for i in range(len(AHEAD_T)) if i not in SWING_T]
-    arrivals += [(texts.leg2[i], BACK_T[i]) for i in range(len(BACK_T))]
-    arrivals += [(texts.straight[i], AHEAD_T[i]) for i in SWING_T]
+    arrivals = list(zip(texts.straight, AHEAD_T)) + list(zip(texts.leg2, BACK_T))
     text_up = [remote(rows(far_text, p), rows(mate_text, p), "mate") for _, p in arrivals]
     ids_up = remote(far_ids, mate_ids, "mate")
     part_over = remote(part, mate_part, "mate")
@@ -308,7 +337,7 @@
     def _():
         carried[...] = (total[...] + accum[...]).astype(jnp.bfloat16)
 
-    pl.semaphore_wait(barrier, 4)
+    pl.semaphore_wait(barrier, partners)
 
     for i in range(max(len(BACK_T), len(AHEAD_T))):
         if i < len(BACK_T):
@@ -335,20 +364,34 @@
         part_over.wait_recv()
         carried[...] = (total[...] + accum[...] + mate_part[...]).astype(jnp.bfloat16)
 
+    @pl.when(short)
+    def _():
+        for copy in carries.help1 or carries.instead:
+            copy.start()
+
     for i in range(len(AHEAD_C)):
         carries.send_ahead(i)
     for i in range(max(len(BACK_T), len(BACK_C))):
         if i < len(BACK_T):
             texts.relay(i)
         if i < len(BACK_C):
-            carries.send_back(i)
-    texts.relay_swing()
+
+            @pl.when(jnp.logical_not(short))
+            def _():
+                carries.leg1[i].start()
+    texts.help()
 
     ids_ahead.wait_recv()
 
     @pl.when(is1)
     def _():
         ids_up.start()
+
+    def relay_carries(first, end):
+        for i in range(first, end):
+            carries.relay(i)
+
+    relay_carries(0, len(BACK_C))
 
     for i, (copy, _) in enumerate(arrivals):
         copy.wait_recv()
@@ -357,9 +400,7 @@
         def _():
             text_up[i].start()
 
-    early = len(BACK_C) // 2
-    for i in range(early):
-        carries.relay(i)
+    carries.help()
 
     @pl.when(is0)
     def _():
@@ -368,10 +409,6 @@
             copy.wait_recv()
         terms(mate_text, mate_ids, False, part)
         part_over.start()
-
-    for i in range(early, len(BACK_C)):
-        carries.relay(i)
-    carries.relay_swing()
 
     terms(far_text, far_ids, False, total)
 
@@ -444,12 +481,12 @@
 
 def solution(mesh):
     dps = mesh.shape["dp"]
-    zs = dps // 8 if dps >= 8 else 1
+    zs = max(dps // 8, 1)
     copies = 3 * len(BACK_T) + 2 * len(AHEAD_T) + len(AHEAD_C) + 2 * len(BACK_C) + 5
-    copies += len(SWING_T) + len(SWING_C)
+    copies += 2
     pieces = len(AHEAD_C) + len(BACK_C)
     passing_rows = sum(n for _, n in BACK_T) + sum(n for _, n in BACK_C)
-    passing_rows += sum(AHEAD_T[i][1] for i in SWING_T) + sum(AHEAD_C[i][1] for i in SWING_C)
+    passing_rows += 32 + 16
 
     def body(image_emb, text_emb, text_accum, pair_ids, log_scale, bias):
         n, d = image_emb.shape

time: 72.3 us -> 63.6 us (0.88)
  the two profiles are of different devices: /device:TPU:10 before, /device:TPU:1 now
where the time goes in v3:
time: 63.6 us; the launch traced here: 63.4 us
  Pallas kernels  59.7 us (94%)
  between operations  1.94 us (3%)
  local copies, waits for them, and re-layouts  1.74 us (3%)
    pallas_call x1, Pallas kernels, body(): pl.pallas_call(functools.partial(kernel, zs, dps), out_shape=shapes, in_s...  58.5 us
    unnamed x4, local copies, waits for them, and re-layouts  1.74 us

profile of v3, /device:TPU:1, one launch (start us, length us, event | category | flops | bytes accessed | tf_op | source)
XLA Modules:
  0.0 63.4 jit_solution(1407096045352825038)
XLA Ops:
  1.9 0.0 copy-start
  1.9 1.1 %copy-done = bf16[256,1152]{1,0:T(8,128)(2,1)S(1)} copy-done((bf16[256,1152]{1,0:T(8,128)(2,1)S(1)}, bf16[256,1152]{1,0:T(8,128)(2,1)}, u32[]{:S(2)}) %copy-start) | copy-done | bytes 589848
  3.0 0.0 copy-start.1
  3.0 0.7 %copy-done.1 = s32[256]{0:T(256)S(1)} copy-done((s32[256]{0:T(256)S(1)}, s32[256]{0:T(256)}, u32[]{:S(2)}) %copy-start.1) | copy-done | bytes 1048
  3.7 58.5 %shard_map.85 = (f32[1,256]{1,0:T(1,128)S(1)}, bf16[256,1152]{1,0:T(8,128)(2,1)S(1)}, f32[256,1152]{1,0:T(8,128)S(1)}) custom-call(f32[1]{0:T(128)S(6)} %copy.9.log_scale_hbm, f32[1]{0:T(128)S(6)} %copy.10.bias_hbm, bf16[256,1152]{1,0:T(8,128)(2,1)S(1)} %copy-done, f32[256,1152]{1,0:T(8,128)} %text_hbm.1, f32[256,1152]{1,0:T(8,128)} %accum_hbm.1, ...), custom_call_target="tpu_custom_call" | custom-call | tf_op jit(solution)/shard_map/pallas_call | solution.py:501
  62.2 1.2 %shard_map.86 = (f32[1,256]{1,0:T(1,128)}, bf16[256,1152]{1,0:T(8,128)(2,1)}, f32[256,1152]{1,0:T(8,128)}) custom-call(f32[1,256]{1,0:T(1,128)S(1)} %get-tuple-element.9.loss, bf16[256,1152]{1,0:T(8,128)(2,1)S(1)} %get-tuple-element.10.image_grad, f32[256,1152]{1,0:T(8,128)S(1)} %get-tuple-element.11.text_grad), custom_call_target="tpu_custom_call" | custom-call | tf_op jit(solution)/shard_map/pallas_call | solution.py:538
Async XLA Ops:
  1.9 1.1 %copy-start = (bf16[256,1152]{1,0:T(8,128)(2,1)S(1)}, bf16[256,1152]{1,0:T(8,128)(2,1)}, u32[]{:S(2)}) copy-start(bf16[256,1152]{1,0:T(8,128)(2,1)} %image_hbm.1) | copy-start | bytes 1769476
  3.0 0.7 %copy-start.1 = (s32[256]{0:T(256)S(1)}, s32[256]{0:T(256)}, u32[]{:S(2)}) copy-start(s32[256]{0:T(256)} %param.9) | copy-start | bytes 3076

commit v4 on v3

--- a/solution.py
+++ b/solution.py
@@ -14,10 +14,11 @@
 
 AHEAD_T = [(64 + 32 * i, 32) for i in range(6)]
 BACK_T = [(16 * i, 16) for i in range(4)]
-AHEAD_C = [(64 + 32 * i, 32) for i in range(5)] + [(224, 16), (240, 16)]
-BACK_C = [(16 * i, 16) for i in range(4)]
-HELP_T = {12: (1, 2, 3, 4, 5, 6, 7, 8, 9, 10)}
-HELP_C = {12: (1, 2, 3, 4)}
+AHEAD_C = [(48, 16)] + [(64 + 32 * i, 32) for i in range(5)] + [(224, 16), (240, 16)]
+BACK_C = [(16 * i, 16) for i in range(3)]
+HELP_T = {12: (1, 2, 3, 4, 5, 6, 7)}
+HELP_C = {12: (1, 2, 3, 4, 5, 6, 7)}
+HELP_T_6 = {12: (1, 2, 3, 4)}
 
 
 def places(zs, dps):
@@ -29,7 +30,7 @@
     y = (group // 2) * 2 + (dp // zs) % 2
     x = dp // (2 * zs)
     last = z == zs - 1
-    helpers = HELP_T.get(zs, ())
+    helpers = (HELP_T_6.get(zs, ()), HELP_T.get(zs, ()))
 
     def chip(x, y, z):
         return ((x * 2 + y % 2) * zs + z, (y // 2) * 2 + core)
@@ -48,12 +49,18 @@
     p_z = p_dp % zs
     p_y = (p_group // 2) * 2 + (p_dp // zs) % 2
     helper = z < 0
-    for z_j in helpers:
-        helper = helper | ((y == 0) & (z == z_j))
+    for low in (0, 1):
+        for z_j in helpers[1 - low]:
+            helper = helper | ((y == low) & (z == z_j))
+    helped = chip(x, 7 - y, zs - 1)
+    p_x = p_dp // (2 * zs)
     return dict(
         core=core,
         z=z,
         short=last & (y == 7),
+        long=last & (y == 6),
+        long_end=(p_z == zs - 1) & (p_y == 6),
+        y=y,
         idle=last & (y == 3),
         end=(p_z == zs - 1) & (p_y == 7),
         late=(p_z == zs - 1) & (p_y >= 6),
@@ -65,10 +72,10 @@
         source=source,
         onward=after(source),
         previous_via=relay(p_dp // (2 * zs), p_y, p_z),
-        helped=chip(x, 7, zs - 1),
-        help_end=chip((x + 1) % xs, 0, 0),
-        helpers=[chip(x, 0, z_j) for z_j in helpers],
-        end_helpers=[chip((x + xs - 1) % xs, 0, z_j) for z_j in helpers],
+        helped=helped,
+        help_end=after(helped),
+        helpers=[[chip(x, 1 - k, z_j) for z_j in zz] for k, zz in enumerate(helpers)],
+        end_helpers=[[chip(p_x, 1 - k, z_j) for z_j in zz] for k, zz in enumerate(helpers)],
     )
 
 
@@ -116,7 +123,7 @@
     is0 = core == 0
     is1 = core == 1
     short, idle, end, helper = at["short"], at["idle"], at["end"], at["helper"]
-    helpers = HELP_T.get(zs, ())
+    helpers = (HELP_T_6.get(zs, ()), HELP_T.get(zs, ()))
     barrier = pltpu.get_barrier_semaphore()
 
     def greet(place):
@@ -133,18 +140,24 @@
     def _():
         greet(at["previous_via"])
 
-    if helpers:
+    if helpers[1]:
+
+        @pl.when(at["long_end"])
+        def _():
+            for place in at["end_helpers"][0]:
+                greet(place)
 
         @pl.when(end)
         def _():
-            for place in at["end_helpers"]:
+            for place in at["end_helpers"][1]:
                 greet(place)
 
         @pl.when(helper)
         def _():
             greet(at["helped"])
 
-    partners = 2 + jnp.where(short, len(helpers), 1) + jnp.where(idle, 0, 1) + jnp.where(helper, 1, 0)
+    partners = 2 + jnp.where(short, len(helpers[1]), 1) + jnp.where(at["long"], len(helpers[0]), 0)
+    partners += jnp.where(idle, 0, 1) + jnp.where(helper, 1, 0)
 
     loads = [
         pltpu.make_async_copy(src, dst, load_sem.at[i])
@@ -189,7 +202,7 @@
         return passing.at[pl.ds(room[0] - n, n)]
 
     class Stream:
-        def __init__(self, src, dst, ahead, back, help_z):
+        def __init__(self, src, dst, ahead, back, help_z, help_z_6=()):
             self.ahead, self.back = ahead, back
             ahead_ids = [fresh() for _ in ahead]
             leg1_ids = [fresh() for _ in back]
@@ -209,29 +222,56 @@
                 for p, k1, k2 in zip(back, leg1_ids, leg2_ids)
             ]
             self.help1, self.help2, self.help_z = [], [], help_z
+            self.six1, self.six2, self.help_z_6 = {}, {}, help_z_6
             if help_z:
                 marks = list(zip(back, leg1_ids, leg2_ids)) + list(zip(ahead, ahead_ids, ahead_ids))
                 marks = marks[: len(help_z)]
                 k, spot = fresh(), room[0]
                 slot(max(p[1] for p, _, _ in marks))
+
+                def pair(p, k1, k2, place):
+                    here = passing.at[pl.ds(spot, p[1])]
+                    return (
+                        remote(rows(src, p), here, place, k1, k),
+                        remote(here, rows(dst, p), "help_end", k, k2),
+                    )
+
                 for j, (p, k1, k2) in enumerate(marks):
-                    here = passing.at[pl.ds(spot, p[1])]
-                    self.help1.append(remote(rows(src, p), here, at["helpers"][j], k1, k))
-                    self.help2.append(remote(here, rows(dst, p), "help_end", k, k2))
-
-        def send_ahead(self, i):
-            if len(self.back) + i < len(self.help1):
-
-                @pl.when(short)
+                    one, two = pair(p, k1, k2, at["helpers"][1][j])
+                    self.help1.append(one)
+                    self.help2.append(two)
+                for j in range(len(help_z_6)):
+                    i = len(ahead) - 1 - j
+                    place = at["helpers"][0][j]
+                    self.six1[i], self.six2[i] = pair(ahead[i], ahead_ids[i], ahead_ids[i], place)
+
+        def send_ahead(self, i, helped=True):
+            straight = None
+            j = len(self.back) + i
+            if j < len(self.help1):
+                straight = jnp.logical_not(short)
+                if helped:
+
+                    @pl.when(short)
+                    def _():
+                        self.help1[j].start()
+
+            if i in self.six1:
+                long = at["long"]
+                other = jnp.logical_not(long)
+                straight = other if straight is None else straight & other
+
+                @pl.when(long)
                 def _():
-                    self.help1[len(self.back) + i].start()
-
-                @pl.when(jnp.logical_not(short))
+                    self.six1[i].start()
+
+            if straight is None:
+                self.straight[i].start()
+            else:
+
+                @pl.when(straight)
                 def _():
                     self.straight[i].start()
-
-            else:
-                self.straight[i].start()
 
         def send_back(self, i):
             @pl.when(short)
@@ -251,7 +291,13 @@
         def each_helper(self, act):
             for z_j, one, two in zip(self.help_z, self.help1, self.help2):
 
-                @pl.when(helper & (at["z"] == z_j))
+                @pl.when((at["y"] == 0) & (at["z"] == z_j))
+                def _():
+                    act(one, two)
+
+            for z_j, one, two in zip(self.help_z_6, self.six1.values(), self.six2.values()):
+
+                @pl.when((at["y"] == 1) & (at["z"] == z_j))
                 def _():
                     act(one, two)
 
@@ -273,7 +319,9 @@
 
             self.each_helper(lambda one, two: two.wait_send())
 
-    texts = Stream(own, far_text, AHEAD_T, BACK_T, HELP_T.get(zs, ()))
+    texts = Stream(
+        own, far_text, AHEAD_T, BACK_T, HELP_T.get(zs, ()), HELP_T_6.get(zs, ())
+    )
     carries = Stream(carried, far_carried, AHEAD_C, BACK_C, HELP_C.get(zs, ()))
     ids_ahead = remote(ids, far_ids, "after")
     text_down = remote(own, mate_text, "mate")
@@ -370,7 +418,7 @@
             copy.start()
 
     for i in range(len(AHEAD_C)):
-        carries.send_ahead(i)
+        carries.send_ahead(i, helped=False)
     for i in range(max(len(BACK_T), len(BACK_C))):
         if i < len(BACK_T):
             texts.relay(i)
@@ -391,7 +439,10 @@
         for i in range(first, end):
             carries.relay(i)
 
-    relay_carries(0, len(BACK_C))
+    half = len(BACK_C) // 2
+    relay_carries(0, half)
+    carries.help()
+    relay_carries(half, len(BACK_C))
 
     for i, (copy, _) in enumerate(arrivals):
         copy.wait_recv()
@@ -399,8 +450,6 @@
         @pl.when(is1)
         def _():
             text_up[i].start()
-
-    carries.help()
 
     @pl.when(is0)
     def _():
@@ -486,7 +535,7 @@
     copies += 2
     pieces = len(AHEAD_C) + len(BACK_C)
     passing_rows = sum(n for _, n in BACK_T) + sum(n for _, n in BACK_C)
-    passing_rows += 32 + 16
+    passing_rows += 32 + 32
 
     def body(image_emb, text_emb, text_accum, pair_ids, log_scale, bias):
         n, d = image_emb.shape

time: 63.6 us -> 59.2 us (0.931)
  Pallas kernels: 59.7 us -> 54.9 us
    pallas_call x1, Pallas kernels: 58.5 us -> 53.7 us  [body(): pl.pallas_call(functools.partial(kernel, zs, dps), out_shape=shapes, in_s...]
where the time goes in v4:
time: 59.2 us; the launch traced here: 58.6 us
  Pallas kernels  54.9 us (93%)
  between operations  1.94 us (3%)
  local copies, waits for them, and re-layouts  1.74 us (3%)
    pallas_call x1, Pallas kernels, body(): pl.pallas_call(functools.partial(kernel, zs, dps), out_shape=shapes, in_s...  53.7 us
    unnamed x4, local copies, waits for them, and re-layouts  1.74 us
    pallas_call x1, Pallas kernels, body(): pl.pallas_call(store_kernel, out_shape=shapes, in_specs=[any_space] * 3,...  1.23 us

profile of v4, /device:TPU:1, one launch (start us, length us, event | category | flops | bytes accessed | tf_op | source)
XLA Modules:
  0.0 58.6 jit_solution(13145021243527384668)
XLA Ops:
  1.9 0.0 copy-start
  1.9 1.1 %copy-done = bf16[256,1152]{1,0:T(8,128)(2,1)S(1)} copy-done((bf16[256,1152]{1,0:T(8,128)(2,1)S(1)}, bf16[256,1152]{1,0:T(8,128)(2,1)}, u32[]{:S(2)}) %copy-start) | copy-done | bytes 589848
  3.0 0.0 copy-start.1
  3.0 0.7 %copy-done.1 = s32[256]{0:T(256)S(1)} copy-done((s32[256]{0:T(256)S(1)}, s32[256]{0:T(256)}, u32[]{:S(2)}) %copy-start.1) | copy-done | bytes 1048
  3.7 53.7 %shard_map.85 = (f32[1,256]{1,0:T(1,128)S(1)}, bf16[256,1152]{1,0:T(8,128)(2,1)S(1)}, f32[256,1152]{1,0:T(8,128)S(1)}) custom-call(f32[1]{0:T(128)S(6)} %copy.9.log_scale_hbm, f32[1]{0:T(128)S(6)} %copy.10.bias_hbm, bf16[256,1152]{1,0:T(8,128)(2,1)S(1)} %copy-done, f32[256,1152]{1,0:T(8,128)} %text_hbm.1, f32[256,1152]{1,0:T(8,128)} %accum_hbm.1, ...), custom_call_target="tpu_custom_call" | custom-call | tf_op jit(solution)/shard_map/pallas_call | solution.py:550
  57.3 1.2 %shard_map.86 = (f32[1,256]{1,0:T(1,128)}, bf16[256,1152]{1,0:T(8,128)(2,1)}, f32[256,1152]{1,0:T(8,128)}) custom-call(f32[1,256]{1,0:T(1,128)S(1)} %get-tuple-element.9.loss, bf16[256,1152]{1,0:T(8,128)(2,1)S(1)} %get-tuple-element.10.image_grad, f32[256,1152]{1,0:T(8,128)S(1)} %get-tuple-element.11.text_grad), custom_call_target="tpu_custom_call" | custom-call | tf_op jit(solution)/shard_map/pallas_call | solution.py:587
Async XLA Ops:
  1.9 1.1 %copy-start = (bf16[256,1152]{1,0:T(8,128)(2,1)S(1)}, bf16[256,1152]{1,0:T(8,128)(2,1)}, u32[]{:S(2)}) copy-start(bf16[256,1152]{1,0:T(8,128)(2,1)} %image_hbm.1) | copy-start | bytes 1769476
  3.0 0.7 %copy-start.1 = (s32[256]{0:T(256)S(1)}, s32[256]{0:T(256)}, u32[]{:S(2)}) copy-start(s32[256]{0:T(256)} %param.9) | copy-start | bytes 3076

commit v5 on v4

--- a/solution.py
+++ b/solution.py
@@ -90,7 +90,8 @@
     ids_hbm,
     loss_hbm,
     image_grad_hbm,
-    text_grad_hbm,
+    text_grad_top,
+    text_grad_bottom,
     image,
     text,
     accum,
@@ -480,9 +481,10 @@
         copy.wait_recv()
         at_rows = pl.ds(piece[0], piece[1])
         total[at_rows, :] = total[at_rows, :] + far_carried[at_rows, :].astype(jnp.float32)
-        store = pltpu.make_async_copy(
-            rows(total, piece), rows(text_grad_hbm, piece), store_sem.at[2 + len(stores)]
-        )
+        middle = total.shape[0] // 2
+        top = piece[0] < middle
+        place = rows(text_grad_top, piece) if top else rows(text_grad_bottom, piece, -middle)
+        store = pltpu.make_async_copy(rows(total, piece), place, store_sem.at[2 + len(stores)])
         store.start()
         stores.append(store)
 
@@ -515,13 +517,15 @@
         store.wait()
 
 
-def store_kernel(loss, image_grad, text_grad, loss_hbm, image_grad_hbm, text_grad_hbm, sem):
-    copies = [
-        pltpu.make_async_copy(src, dst, sem.at[i])
-        for i, (src, dst) in enumerate(
-            [(text_grad, text_grad_hbm), (image_grad, image_grad_hbm), (loss, loss_hbm)]
-        )
+def store_kernel(loss, image_grad, top, bottom, loss_hbm, image_grad_hbm, text_grad_hbm, sem):
+    middle = top.shape[0]
+    pairs = [
+        (top, text_grad_hbm.at[pl.ds(0, middle)]),
+        (bottom, text_grad_hbm.at[pl.ds(middle, middle)]),
+        (image_grad, image_grad_hbm),
+        (loss, loss_hbm),
     ]
+    copies = [pltpu.make_async_copy(src, dst, sem.at[i]) for i, (src, dst) in enumerate(pairs)]
     for copy in copies:
         copy.start()
     for copy in copies:
@@ -549,9 +553,9 @@
         )
         results = pl.pallas_call(
             functools.partial(kernel, zs, dps),
-            out_shape=shapes,
+            out_shape=shapes[:2] + (jax.ShapeDtypeStruct((n // 2, d), f32),) * 2,
             in_specs=[hbm] * 6,
-            out_specs=(any_space, any_space, any_space),
+            out_specs=(any_space,) * 4,
             scratch_shapes=[
                 pltpu.VMEM((n, d), bf16),
                 pltpu.VMEM((n, d), f32),
@@ -581,15 +585,15 @@
                 pltpu.SemaphoreType.DMA((copies,)),
             ],
             compiler_params=pltpu.CompilerParams(
-                collective_id=0, has_side_effects=True, vmem_limit_bytes=51 << 20
+                collective_id=0, has_side_effects=True, vmem_limit_bytes=53120 << 10
             ),
         )(log_scale, bias, image_emb, text_emb, text_accum, pair_ids.reshape(1, n))
         loss, image_grad, text_grad = pl.pallas_call(
             store_kernel,
             out_shape=shapes,
-            in_specs=[any_space] * 3,
+            in_specs=[any_space] * 4,
             out_specs=(hbm, hbm, hbm),
-            scratch_shapes=[pltpu.SemaphoreType.DMA((3,))],
+            scratch_shapes=[pltpu.SemaphoreType.DMA((4,))],
             compiler_params=pltpu.CompilerParams(vmem_limit_bytes=1 << 20),
         )(*results)
         return loss.reshape(n), image_grad, text_grad

time: 59.2 us -> 58.3 us (0.985)
  local copies, waits for them, and re-layouts: 1.74 us -> 0.67 us
    unnamed x4 -> x2, local copies, waits for them, and re-layouts: 1.74 us -> 0.67 us
where the time goes in v5:
time: 58.3 us; the launch traced here: 57.6 us
  Pallas kernels  55 us (94%)
  between operations  1.94 us (3%)
  local copies, waits for them, and re-layouts  0.67 us (1%)
    pallas_call x1, Pallas kernels, body(): pl.pallas_call(functools.partial(kernel, zs, dps), out_shape=shapes[:2] +...  53.7 us
    pallas_call x1, Pallas kernels, body(): pl.pallas_call(store_kernel, out_shape=shapes, in_specs=[any_space] * 4,...  1.24 us

profile of v5, /device:TPU:1, one launch (start us, length us, event | category | flops | bytes accessed | tf_op | source)
XLA Modules:
  0.0 57.6 jit_solution(17844687056880041481)
XLA Ops:
  1.9 0.0 copy-start
  1.9 0.7 %copy-done = s32[256]{0:T(256)S(1)} copy-done((s32[256]{0:T(256)S(1)}, s32[256]{0:T(256)}, u32[]{:S(2)}) %copy-start) | copy-done | bytes 1048
  2.6 53.7 %shard_map.85 = (f32[1,256]{1,0:T(1,128)S(1)}, bf16[256,1152]{1,0:T(8,128)(2,1)S(1)}, f32[128,1152]{1,0:T(8,128)S(1)}, f32[128,1152]{1,0:T(8,128)S(1)}) custom-call(f32[1]{0:T(128)S(6)} %copy.9.log_scale_hbm, f32[1]{0:T(128)S(6)} %copy.10.bias_hbm, bf16[256,1152]{1,0:T(8,128)(2,1)} %image_hbm.1, f32[256,1152]{1,0:T(8,128)} %text_hbm.1, ...), custom_call_target="tpu_custom_call" | custom-call | tf_op jit(solution)/shard_map/pallas_call | solution.py:554
  56.4 1.2 %shard_map.86 = (f32[1,256]{1,0:T(1,128)}, bf16[256,1152]{1,0:T(8,128)(2,1)}, f32[256,1152]{1,0:T(8,128)}) custom-call(f32[1,256]{1,0:T(1,128)S(1)} %get-tuple-element.10.loss, bf16[256,1152]{1,0:T(8,128)(2,1)S(1)} %get-tuple-element.11.image_grad, f32[128,1152]{1,0:T(8,128)S(1)} %get-tuple-element.12.top, f32[128,1152]{1,0:T(8,128)S(1)} %get-tuple-element.13.bottom), custom_call_target="tpu_custom_call" | custom-call | tf_op jit(solution)/shard_map/pallas_call | solution.py:591
Async XLA Ops:
  1.9 0.7 %copy-start = (s32[256]{0:T(256)S(1)}, s32[256]{0:T(256)}, u32[]{:S(2)}) copy-start(s32[256]{0:T(256)} %param.9) | copy-start | bytes 3076

commit v6 on v5

--- a/solution.py
+++ b/solution.py
@@ -19,6 +19,7 @@
 HELP_T = {12: (1, 2, 3, 4, 5, 6, 7)}
 HELP_C = {12: (1, 2, 3, 4, 5, 6, 7)}
 HELP_T_6 = {12: (1, 2, 3, 4)}
+HELP_C_6 = {12: (1, 2, 3)}
 
 
 def places(zs, dps):
@@ -323,7 +324,9 @@
     texts = Stream(
         own, far_text, AHEAD_T, BACK_T, HELP_T.get(zs, ()), HELP_T_6.get(zs, ())
     )
-    carries = Stream(carried, far_carried, AHEAD_C, BACK_C, HELP_C.get(zs, ()))
+    carries = Stream(
+        carried, far_carried, AHEAD_C, BACK_C, HELP_C.get(zs, ()), HELP_C_6.get(zs, ())
+    )
     ids_ahead = remote(ids, far_ids, "after")
     text_down = remote(own, mate_text, "mate")
     ids_down = remote(ids, mate_ids, "mate")

time: 58.3 us -> 57.8 us (level)
  no operation moved by 1% of the time
where the time goes in v6:
time: 57.8 us; the launch traced here: 57.6 us
  Pallas kernels  55 us (95%)
  between operations  1.94 us (3%)
  local copies, waits for them, and re-layouts  0.67 us (1%)
    pallas_call x1, Pallas kernels, body(): pl.pallas_call(functools.partial(kernel, zs, dps), out_shape=shapes[:2] +...  53.7 us
    pallas_call x1, Pallas kernels, body(): pl.pallas_call(store_kernel, out_shape=shapes, in_specs=[any_space] * 4,...  1.24 us

profile of v6, /device:TPU:1, one launch (start us, length us, event | category | flops | bytes accessed | tf_op | source)
XLA Modules:
  0.0 57.6 jit_solution(767058841261132745)
XLA Ops:
  1.9 0.0 copy-start
  1.9 0.7 %copy-done = s32[256]{0:T(256)S(1)} copy-done((s32[256]{0:T(256)S(1)}, s32[256]{0:T(256)}, u32[]{:S(2)}) %copy-start) | copy-done | bytes 1048
  2.6 53.7 %shard_map.85 = (f32[1,256]{1,0:T(1,128)S(1)}, bf16[256,1152]{1,0:T(8,128)(2,1)S(1)}, f32[128,1152]{1,0:T(8,128)S(1)}, f32[128,1152]{1,0:T(8,128)S(1)}) custom-call(f32[1]{0:T(128)S(6)} %copy.9.log_scale_hbm, f32[1]{0:T(128)S(6)} %copy.10.bias_hbm, bf16[256,1152]{1,0:T(8,128)(2,1)} %image_hbm.1, f32[256,1152]{1,0:T(8,128)} %text_hbm.1, ...), custom_call_target="tpu_custom_call" | custom-call | tf_op jit(solution)/shard_map/pallas_call | solution.py:557
  56.3 1.2 %shard_map.86 = (f32[1,256]{1,0:T(1,128)}, bf16[256,1152]{1,0:T(8,128)(2,1)}, f32[256,1152]{1,0:T(8,128)}) custom-call(f32[1,256]{1,0:T(1,128)S(1)} %get-tuple-element.10.loss, bf16[256,1152]{1,0:T(8,128)(2,1)S(1)} %get-tuple-element.11.image_grad, f32[128,1152]{1,0:T(8,128)S(1)} %get-tuple-element.12.top, f32[128,1152]{1,0:T(8,128)S(1)} %get-tuple-element.13.bottom), custom_call_target="tpu_custom_call" | custom-call | tf_op jit(solution)/shard_map/pallas_call | solution.py:594
Async XLA Ops:
  1.9 0.7 %copy-start = (s32[256]{0:T(256)S(1)}, s32[256]{0:T(256)}, u32[]{:S(2)}) copy-start(s32[256]{0:T(256)} %param.9) | copy-start | bytes 3076

commit v7 on v6

--- a/solution.py
+++ b/solution.py
@@ -17,7 +17,7 @@
 AHEAD_C = [(48, 16)] + [(64 + 32 * i, 32) for i in range(5)] + [(224, 16), (240, 16)]
 BACK_C = [(16 * i, 16) for i in range(3)]
 HELP_T = {12: (1, 2, 3, 4, 5, 6, 7)}
-HELP_C = {12: (1, 2, 3, 4, 5, 6, 7)}
+HELP_C = {12: (1, 2, 3, 4, 5, 6)}
 HELP_T_6 = {12: (1, 2, 3, 4)}
 HELP_C_6 = {12: (1, 2, 3)}
 

time: 57.8 us -> 57.7 us (level); the launches traced: 57.6 us -> 56.8 us
  Pallas kernels: 55 us -> 54.2 us
    pallas_call x1, Pallas kernels: 53.7 us -> 52.9 us  [body(): pl.pallas_call(functools.partial(kernel, zs, dps), out_shape=shapes[:2] +...]
where the time goes in v7:
time: 57.7 us; the launch traced here: 56.8 us
  Pallas kernels  54.2 us (94%)
  between operations  1.94 us (3%)
  local copies, waits for them, and re-layouts  0.67 us (1%)
    pallas_call x1, Pallas kernels, body(): pl.pallas_call(functools.partial(kernel, zs, dps), out_shape=shapes[:2] +...  52.9 us
    pallas_call x1, Pallas kernels, body(): pl.pallas_call(store_kernel, out_shape=shapes, in_specs=[any_space] * 4,...  1.24 us

profile of v7, /device:TPU:1, one launch (start us, length us, event | category | flops | bytes accessed | tf_op | source)
XLA Modules:
  0.0 56.8 jit_solution(13989625530113352997)
XLA Ops:
  1.9 0.0 copy-start
  1.9 0.7 %copy-done = s32[256]{0:T(256)S(1)} copy-done((s32[256]{0:T(256)S(1)}, s32[256]{0:T(256)}, u32[]{:S(2)}) %copy-start) | copy-done | bytes 1048
  2.6 52.9 %shard_map.85 = (f32[1,256]{1,0:T(1,128)S(1)}, bf16[256,1152]{1,0:T(8,128)(2,1)S(1)}, f32[128,1152]{1,0:T(8,128)S(1)}, f32[128,1152]{1,0:T(8,128)S(1)}) custom-call(f32[1]{0:T(128)S(6)} %copy.9.log_scale_hbm, f32[1]{0:T(128)S(6)} %copy.10.bias_hbm, bf16[256,1152]{1,0:T(8,128)(2,1)} %image_hbm.1, f32[256,1152]{1,0:T(8,128)} %text_hbm.1, ...), custom_call_target="tpu_custom_call" | custom-call | tf_op jit(solution)/shard_map/pallas_call | solution.py:557
  55.5 1.2 %shard_map.86 = (f32[1,256]{1,0:T(1,128)}, bf16[256,1152]{1,0:T(8,128)(2,1)}, f32[256,1152]{1,0:T(8,128)}) custom-call(f32[1,256]{1,0:T(1,128)S(1)} %get-tuple-element.10.loss, bf16[256,1152]{1,0:T(8,128)(2,1)S(1)} %get-tuple-element.11.image_grad, f32[128,1152]{1,0:T(8,128)S(1)} %get-tuple-element.12.top, f32[128,1152]{1,0:T(8,128)S(1)} %get-tuple-element.13.bottom), custom_call_target="tpu_custom_call" | custom-call | tf_op jit(solution)/shard_map/pallas_call | solution.py:594
Async XLA Ops:
  1.9 0.7 %copy-start = (s32[256]{0:T(256)S(1)}, s32[256]{0:T(256)}, u32[]{:S(2)}) copy-start(s32[256]{0:T(256)} %param.9) | copy-start | bytes 3076
